TPU v7x, 32 devices: a whole 2x2x4 slice. The times are simulated.
32 devices in a mesh: gx: 8 (over z, y), gy: 4 (over x, core).
Axes of the slice: x: 2, y: 2, z: 4, core: 2. Of those that a mesh axis runs over, the one named last changes fastest.
Arguments:
- ocean_current: float32 [2, 256, 2048], P(None, 'gx', 'gy'), may hold values from -6 to 6
- floe_state: float32 [1024, 4, 128], P(('gx', 'gy')), may hold values from -6 to 6
- floe_source: int32 [1024, 1], P(('gx', 'gy')), may hold values from 0 to 31; in each aligned block of 32 rows (0 to 31, 32 to 63, ...) at most 2 rows name the same one
- floe_patch: int32 [1024, 1], P(('gx', 'gy')), may hold values from 0 to 63
- floe_cell: int32 [1024, 2, 128], P(('gx', 'gy')), may hold values from 0 to 14
- floe_frac: float32 [1024, 2, 128], P(('gx', 'gy')), may hold values from 0 to 1
- bond_blocks: int32 [1024, 2, 4], P(('gx', 'gy')), may hold values from 0 to 31, as said below
- bond_lanes: int32 [1024, 4, 128], P(('gx', 'gy')), may hold values from 0 to 127
- bond_stiff: float32 [1024, 4, 128], P(('gx', 'gy')), may hold values from 0.5 to 2
- contact_blocks: int32 [1024, 2, 4], P(('gx', 'gy')), may hold values from 0 to 31, as said below
- contact_lanes: int32 [1024, 4, 128], P(('gx', 'gy')), may hold values from 0 to 127
Outputs:
- floe_final: float32 [1024, 4, 128], P(('gx', 'gy'))
- ocean_stress: float32 [2, 256, 2048], P(None, 'gx', 'gy')
Inputs may be any that keep to these rules, and one draw needn't show every extreme that they name: `floe_source`: the blocks of one region name one tile at most 2 times; in every region some tile is named exactly 2 times. bond_blocks[k, 0, s] is a region code 0 to 4; bond_blocks[k, 1, s] is below 32 where the code is 0, else below 16. contact_blocks[k, 0, s] is a region code 0 to 4; contact_blocks[k, 1, s] is below 32 where the code is 0, else below 16.
All inputs are finite; a program needn't handle non-finite values.
Results may differ from a plain program's by a relative error of at most 0.00012.
Values sent between devices are 32-bit elements; how exact they have to be, the bound alone decides.
A program may use at most 64 MiB of HBM per device.

v0:
```python
import jax
import jax.numpy as jnp
from jax import lax
from jax.sharding import PartitionSpec as P

PS = 16
EDGE = 16
NB = 4
SUBSTEPS = 4


HIGH = lax.Precision.HIGHEST


def extended(value, sides, width):
    for axis, dim in sides:
        size, length = (lax.axis_size(axis), value.shape[dim])
        up = [(i, (i + 1) % size) for i in range(size)]
        down = [(j, i) for i, j in up]
        last = lax.slice_in_dim(value, length - width, length, axis=dim)
        initial = lax.slice_in_dim(value, 0, width, axis=dim)
        before = lax.ppermute(last, axis, up)
        after = lax.ppermute(initial, axis, down)
        value = jnp.concatenate([before, value, after], axis=dim)
    return value


def weights(cell, frac):
    ticks = jnp.arange(PS, dtype=jnp.int32)[None, :, None]
    col_i = cell[:, 0, None, :]
    row_j = cell[:, 1, None, :]
    frac_x = frac[:, 0, None, :]
    frac_y = frac[:, 1, None, :]
    col_weight = (1.0 - frac_x) * (ticks == col_i) + frac_x * (ticks == col_i + 1)
    row_weight = (1.0 - frac_y) * (ticks == row_j) + frac_y * (ticks == row_j + 1)
    return (col_weight, row_weight)


def sample(patch, col_weight, row_weight):
    values = patch.reshape(patch.shape[0], 2, PS, PS)
    inner = jnp.einsum("kcab,kbf->kcaf", values, row_weight, precision=HIGH)
    return jnp.sum(col_weight[:, None] * inner, axis=2)


def deposit(stress, col_weight, row_weight):
    spread = col_weight[:, None] * stress[:, :, None, :]
    result = jnp.einsum("kcaf,kbf->kcab", spread, row_weight, precision=HIGH)
    return result.reshape(stress.shape[0], 2, PS * PS)


def pick_lanes(partner_blocks, lanes):
    blocks = partner_blocks.shape[0]
    slots = partner_blocks.shape[1]
    width = partner_blocks.shape[3]
    grouped_rows = partner_blocks.reshape(blocks // 2, 2, slots, 4, width)
    grouped_lanes = lanes.reshape(blocks // 2, 2, slots, width)

    def select(items):
        rows_here, lanes_here = items
        ticks = jnp.arange(width, dtype=jnp.int32)[None, None, :, None]
        picker = (lanes_here[:, :, None, :] == ticks).astype(jnp.float32)
        return jnp.einsum("kscg,ksgf->kscf", rows_here, picker, precision=HIGH)

    picked = lax.map(select, (grouped_rows, grouped_lanes))
    return picked.reshape(blocks, slots, 4, width)


def interact(own, partner, stiff, current):
    dx = partner[:, :, 0] - own[:, None, 0]
    dy = partner[:, :, 1] - own[:, None, 1]
    du = partner[:, :, 2] - own[:, None, 2]
    dv = partner[:, :, 3] - own[:, None, 3]
    bond_x = jnp.sum(stiff * dx[:, :NB] + 0.2 * du[:, :NB], axis=1)
    bond_y = jnp.sum(stiff * dy[:, :NB] + 0.2 * dv[:, :NB], axis=1)
    near_x = dx[:, NB:]
    near_y = dy[:, NB:]
    dist = jnp.sqrt(near_x * near_x + near_y * near_y)
    push = 2.0 * jnp.maximum(1.5 - dist, 0.0) / jnp.maximum(dist, 0.5)
    touch_x = -jnp.sum(push * near_x, axis=1)
    touch_y = -jnp.sum(push * near_y, axis=1)
    slip_x = current[:, 0] - own[:, 2]
    slip_y = current[:, 1] - own[:, 3]
    speed = jnp.sqrt(slip_x * slip_x + slip_y * slip_y)
    drag_x = 0.5 * speed * slip_x
    drag_y = 0.5 * speed * slip_y
    new_u = own[:, 2] + 0.05 * (bond_x + touch_x + drag_x)
    new_v = own[:, 3] + 0.05 * (bond_y + touch_y + drag_y)
    new_x = own[:, 0] + 0.05 * new_u
    new_y = own[:, 1] + 0.05 * new_v
    return (jnp.stack([new_x, new_y, new_u, new_v], axis=1), jnp.stack([drag_x, drag_y], axis=1))


def route_requests(wanted):
    return lax.all_to_all(wanted, ("gx", "gy"), split_axis=0, concat_axis=0, tiled=True)


def route_currents(served):
    return lax.all_to_all(served, ("gx", "gy"), split_axis=0, concat_axis=0, tiled=True)


def route_stress(returned):
    return lax.all_to_all(returned, ("gx", "gy"), split_axis=0, concat_axis=0, tiled=True)


def local(
    ocean_current,
    floe_state,
    floe_source,
    floe_patch,
    floe_cell,
    floe_frac,
    bond_blocks,
    bond_lanes,
    bond_stiff,
    contact_blocks,
    contact_lanes,
):
    cols = lax.axis_size("gx")
    rows = lax.axis_size("gy")
    devices = cols * rows
    blocks = floe_state.shape[0]
    lane_count = floe_state.shape[2]
    capacity = max(2, 2 * blocks // devices)
    tile_x = ocean_current.shape[1]
    tile_y = ocean_current.shape[2]
    npx = tile_x // PS
    npy = tile_y // PS
    patches = (
        ocean_current.reshape(2, npx, PS, npy, PS)
        .transpose(1, 3, 0, 2, 4)
        .reshape(npx * npy, 2, PS * PS)
    )
    source = floe_source[:, 0]
    wanted = floe_patch[:, 0]
    marks = (source[:, None] == jnp.arange(devices, dtype=jnp.int32)[None, :]).astype(jnp.int32)
    rank = jnp.sum(marks * jnp.cumsum(marks, axis=0), axis=1) - 1
    requests = jnp.zeros((devices, capacity), jnp.int32).at[source, rank].set(wanted + 1)
    served_ids = route_requests(requests)
    live = (served_ids > 0).astype(jnp.float32)
    outgoing = patches[jnp.maximum(served_ids - 1, 0)] * live[:, :, None, None]
    incoming = route_currents(outgoing)
    mine = incoming[source, rank]
    col_weight, row_weight = weights(floe_cell, floe_frac)
    current = sample(mine, col_weight, row_weight)
    region = jnp.concatenate([bond_blocks[:, 0], contact_blocks[:, 0]], axis=1)
    number = jnp.concatenate([bond_blocks[:, 1], contact_blocks[:, 1]], axis=1)
    starts = jnp.array([EDGE, 0, EDGE + blocks, 2 * EDGE + blocks, 3 * EDGE + blocks], jnp.int32)
    codes = (region[:, :, None] == jnp.arange(5, dtype=jnp.int32)[None, None, :]).astype(jnp.int32)
    pool_index = jnp.sum(codes * starts[None, None, :], axis=2) + number
    lanes = jnp.concatenate([bond_lanes, contact_lanes], axis=1)
    state = floe_state
    drag_total = jnp.zeros((blocks, 2, lane_count), jnp.float32)
    for step in range(SUBSTEPS):
        across = extended(state, (("gx", 0),), EDGE)
        along = extended(state, (("gy", 0),), EDGE)
        pool = jnp.concatenate([across, along[:EDGE], along[EDGE + blocks :]], axis=0)
        partner = pick_lanes(pool[pool_index], lanes)
        state, drag = interact(state, partner, bond_stiff, current)
        drag_total = drag_total + drag
    floe_stress = -drag_total / SUBSTEPS
    pieces = deposit(floe_stress, col_weight, row_weight)
    returned = jnp.zeros((devices, capacity, 2, PS * PS), jnp.float32).at[source, rank].set(pieces)
    arrived = route_stress(returned)
    owners = (
        (served_ids.reshape(-1) - 1)[None, :] == jnp.arange(npx * npy, dtype=jnp.int32)[:, None]
    ).astype(jnp.float32)
    summed = jnp.dot(owners, arrived.reshape(devices * capacity, 2 * PS * PS), precision=HIGH)
    ocean_stress = (
        summed.reshape(npx, npy, 2, PS, PS).transpose(2, 0, 3, 1, 4).reshape(2, tile_x, tile_y)
    )
    return (state, ocean_stress)


def solution(mesh):
    in_specs = (
        P(None, "gx", "gy"),
        P(("gx", "gy"), None, None),
        P(("gx", "gy"), None),
        P(("gx", "gy"), None),
        P(("gx", "gy"), None, None),
        P(("gx", "gy"), None, None),
        P(("gx", "gy"), None, None),
        P(("gx", "gy"), None, None),
        P(("gx", "gy"), None, None),
        P(("gx", "gy"), None, None),
        P(("gx", "gy"), None, None),
    )
    out_specs = (P(("gx", "gy"), None, None), P(None, "gx", "gy"))
    return jax.shard_map(local, mesh=mesh, in_specs=in_specs, out_specs=out_specs, check_vma=False)
```

profile of v0, /device:TPU:0, one launch (start us, length us, event | category | flops | bytes accessed | tf_op | source)
XLA Modules:
  0.0 125.3 jit_solution(17001816043622092582)
XLA Ops:
  0.6 0.8 fusion.84
  1.4 3.0 %collective-permute-start = (f32[16,4,128]{2,1,0:T(4,128)S(1)}, f32[16,4,128]{2,1,0:T(4,128)S(1)}, u32[]{:S(2)}, u32[]{:S(2)}) collective-permute-start(f32[16,4,128]{2,1,0:T(4,128)S(1)} %get-tuple-element.207), channel_id=1, source_target_pairs={{0,4},{4,8},{8,12},{12,16},{16,20},{20,24},{24,28},{28,0},{1,5},{5... | collective-permute-start | bytes 98312 | tf_op jit(solution)/shard_map/ppermute | solution.py:22
  4.4 3.2 %collective-permute-start.1 = (f32[16,4,128]{2,1,0:T(4,128)S(1)}, f32[16,4,128]{2,1,0:T(4,128)S(1)}, u32[]{:S(2)}, u32[]{:S(2)}) collective-permute-start(f32[16,4,128]{2,1,0:T(4,128)S(1)} %get-tuple-element.206), channel_id=1, source_target_pairs={{4,0},{8,4},{12,8},{16,12},{20,16},{24,20},{28,24},{0,28},{5,1},{9... | collective-permute-start | bytes 98312 | tf_op jit(solution)/shard_map/ppermute | solution.py:23
  7.5 1.4 %collective-permute-start.3 = (f32[16,4,128]{2,1,0:T(4,128)S(1)}, f32[16,4,128]{2,1,0:T(4,128)S(1)}, u32[]{:S(2)}, u32[]{:S(2)}) collective-permute-start(f32[16,4,128]{2,1,0:T(4,128)S(1)} %get-tuple-element.206), channel_id=1, source_target_pairs={{1,0},{2,1},{3,2},{0,3},{5,4},{6,5},{7,6},{4,7},{9,8},{10,9},{11,1... | collective-permute-start | bytes 98312 | tf_op jit(solution)/shard_map/ppermute | solution.py:23
  10.6 2.0 %scatter_fusion = s32[32,2]{0,1:T(2,128)S(1)} fusion(s32[32,2]{0,1:T(2,128)S(1)} %broadcast.376, s32[32]{0:T(128)S(1)} %get-tuple-element.178, s32[32]{0:T(128)S(1)} %add_bitcast_fusion), kind=kCustom, calls=%fused_computation.6 | custom fusion | bytes 640 | tf_op jit(solution)/shard_map/scatter | solution.py:137
  13.3 3.3 %all-to-all-start = ((s32[32,1,2]{2,1,0:T(1,128)}), s32[32,1,2]{2,1,0:T(1,128)S(1)}, u32[]{:S(2)}, u32[]{:S(2)}) async-start(s32[32,1,2]{2,1,0:T(1,128)} %copy.152), calls=%async_computation | async-start | bytes 32768 | tf_op jit(solution)/shard_map/all_to_all | solution.py:94
  20.4 0.8 copy-done.2
  22.4 1.2 all-to-all-done
  24.7 0.8 broadcast_multiply_fusion
  25.5 4.6 %all-to-all-start.1 = ((f32[32,2,2,256]{3,2,1,0:T(2,128)}), f32[32,2,2,256]{3,2,1,0:T(2,128)S(1)}, u32[]{:S(2)}, u32[]{:S(2)}) async-start(f32[32,2,2,256]{3,2,1,0:T(2,128)} %broadcast_multiply_fusion), calls=%async_computation.1 | async-start | bytes 262144 | tf_op jit(solution)/shard_map/all_to_all | solution.py:98
  30.3 1.0 gather_fusion
  31.4 9.6 %while.40 = (s32[]{:T(128)}, f32[16,2,8,4,128]{4,3,2,1,0:T(4,128)S(1)}, f32[16,2,8,4,128]{4,3,2,1,0:T(4,128)S(1)}, s32[16,2,8,128]{3,2,1,0:T(8,128)S(1)}, s32[]{:T(128)}) while((s32[]{:T(128)}, f32[16,2,8,4,128]{4,3,2,1,0:T(4,128)S(1)}, f32[16,2,8,4,128]{4,3,2,1,0:T(4,128)S(1)}, s32[16,2,8,128]{3,2,1,0:T(8,128)S(1)}, s32[]{:T(128)}) %tuple.145), condition=%wide.region_2.3_spmd, body=%wide.region_1.2_spmd.sunk | while | flops 12845058 | bytes 91201 | solution.py:64
  41.4 0.8 copy-done.1
  44.9 1.8 %collective-permute-start.4 = (f32[16,4,128]{2,1,0:T(4,128)S(1)}, f32[16,4,128]{2,1,0:T(4,128)S(1)}, u32[]{:S(2)}, u32[]{:S(2)}) collective-permute-start(f32[16,4,128]{2,1,0:T(4,128)S(1)} %get-tuple-element.201), channel_id=1, source_target_pairs={{0,4},{4,8},{8,12},{12,16},{16,20},{20,24},{24,28},{28,0},{1,5},{5... | collective-permute-start | bytes 98312 | tf_op jit(solution)/shard_map/ppermute | solution.py:22
  46.7 3.0 %collective-permute-start.5 = (f32[16,4,128]{2,1,0:T(4,128)S(1)}, f32[16,4,128]{2,1,0:T(4,128)S(1)}, u32[]{:S(2)}, u32[]{:S(2)}) collective-permute-start(f32[16,4,128]{2,1,0:T(4,128)S(1)} %get-tuple-element.200), channel_id=1, source_target_pairs={{4,0},{8,4},{12,8},{16,12},{20,16},{24,20},{28,24},{0,28},{5,1},{9... | collective-permute-start | bytes 98312 | tf_op jit(solution)/shard_map/ppermute | solution.py:23
  49.7 1.4 %collective-permute-start.7 = (f32[16,4,128]{2,1,0:T(4,128)S(1)}, f32[16,4,128]{2,1,0:T(4,128)S(1)}, u32[]{:S(2)}, u32[]{:S(2)}) collective-permute-start(f32[16,4,128]{2,1,0:T(4,128)S(1)} %get-tuple-element.200), channel_id=1, source_target_pairs={{1,0},{2,1},{3,2},{0,3},{5,4},{6,5},{7,6},{4,7},{9,8},{10,9},{11,1... | collective-permute-start | bytes 98312 | tf_op jit(solution)/shard_map/ppermute | solution.py:23
  51.7 1.0 collective-permute-done.7
  52.7 1.0 gather_fusion.3
  53.8 9.6 %while.41 = (s32[]{:T(128)}, f32[16,2,8,4,128]{4,3,2,1,0:T(4,128)S(1)}, f32[16,2,8,4,128]{4,3,2,1,0:T(4,128)S(1)}, s32[16,2,8,128]{3,2,1,0:T(8,128)S(1)}, s32[]{:T(128)}) while((s32[]{:T(128)}, f32[16,2,8,4,128]{4,3,2,1,0:T(4,128)S(1)}, f32[16,2,8,4,128]{4,3,2,1,0:T(4,128)S(1)}, s32[16,2,8,128]{3,2,1,0:T(8,128)S(1)}, s32[]{:T(128)}) %tuple.146), condition=%wide.region_12.13_spmd, body=%wide.region_11.12_spmd.sunk | while | flops 12845058 | bytes 91201 | solution.py:64
  64.8 1.6 %collective-permute-start.10 = (f32[16,4,128]{2,1,0:T(4,128)S(1)}, f32[16,4,128]{2,1,0:T(4,128)S(1)}, u32[]{:S(2)}, u32[]{:S(2)}) collective-permute-start(f32[16,4,128]{2,1,0:T(4,128)S(1)} %get-tuple-element.199), channel_id=1, source_target_pairs={{0,1},{1,2},{2,3},{3,0},{4,5},{5,6},{6,7},{7,4},{8,9},{9,10},{10,1... | collective-permute-start | bytes 98312 | tf_op jit(solution)/shard_map/ppermute | solution.py:22
  66.4 4.4 %collective-permute-start.9 = (f32[16,4,128]{2,1,0:T(4,128)S(1)}, f32[16,4,128]{2,1,0:T(4,128)S(1)}, u32[]{:S(2)}, u32[]{:S(2)}) collective-permute-start(f32[16,4,128]{2,1,0:T(4,128)S(1)} %get-tuple-element.198), channel_id=1, source_target_pairs={{4,0},{8,4},{12,8},{16,12},{20,16},{24,20},{28,24},{0,28},{5,1},{9... | collective-permute-start | bytes 98312 | tf_op jit(solution)/shard_map/ppermute | solution.py:23
  71.2 1.2 collective-permute-done.9
  72.5 1.0 gather_fusion.4
  73.6 9.6 %while.42 = (s32[]{:T(128)}, f32[16,2,8,4,128]{4,3,2,1,0:T(4,128)S(1)}, f32[16,2,8,4,128]{4,3,2,1,0:T(4,128)S(1)}, s32[16,2,8,128]{3,2,1,0:T(8,128)S(1)}, s32[]{:T(128)}) while((s32[]{:T(128)}, f32[16,2,8,4,128]{4,3,2,1,0:T(4,128)S(1)}, f32[16,2,8,4,128]{4,3,2,1,0:T(4,128)S(1)}, s32[16,2,8,128]{3,2,1,0:T(8,128)S(1)}, s32[]{:T(128)}) %tuple.147), condition=%wide.region_18.19_spmd, body=%wide.region_17.18_spmd.sunk | while | flops 12845058 | bytes 91201 | solution.py:64
  84.3 1.8 %collective-permute-start.14 = (f32[16,4,128]{2,1,0:T(4,128)S(1)}, f32[16,4,128]{2,1,0:T(4,128)S(1)}, u32[]{:S(2)}, u32[]{:S(2)}) collective-permute-start(f32[16,4,128]{2,1,0:T(4,128)S(1)} %get-tuple-element.197), channel_id=1, source_target_pairs={{0,1},{1,2},{2,3},{3,0},{4,5},{5,6},{6,7},{7,4},{8,9},{9,10},{10,1... | collective-permute-start | bytes 98312 | tf_op jit(solution)/shard_map/ppermute | solution.py:22
  86.0 4.4 %collective-permute-start.13 = (f32[16,4,128]{2,1,0:T(4,128)S(1)}, f32[16,4,128]{2,1,0:T(4,128)S(1)}, u32[]{:S(2)}, u32[]{:S(2)}) collective-permute-start(f32[16,4,128]{2,1,0:T(4,128)S(1)} %get-tuple-element.196), channel_id=1, source_target_pairs={{4,0},{8,4},{12,8},{16,12},{20,16},{24,20},{28,24},{0,28},{5,1},{9... | collective-permute-start | bytes 98312 | tf_op jit(solution)/shard_map/ppermute | solution.py:23
  92.4 1.0 gather_fusion.5
  93.5 9.6 %while.43 = (s32[]{:T(128)}, f32[16,2,8,4,128]{4,3,2,1,0:T(4,128)S(1)}, f32[16,2,8,4,128]{4,3,2,1,0:T(4,128)S(1)}, s32[16,2,8,128]{3,2,1,0:T(8,128)S(1)}, s32[]{:T(128)}) while((s32[]{:T(128)}, f32[16,2,8,4,128]{4,3,2,1,0:T(4,128)S(1)}, f32[16,2,8,4,128]{4,3,2,1,0:T(4,128)S(1)}, s32[16,2,8,128]{3,2,1,0:T(8,128)S(1)}, s32[]{:T(128)}) %tuple.144), condition=%wide.region_24.25_spmd, body=%wide.region_23.24_spmd.sunk | while | flops 12845058 | bytes 91201 | solution.py:64
  105.9 3.8 %scatter_fusion.1 = f32[32,2,2,256]{3,2,1,0:T(2,128)} fusion(f32[32,2,2,256]{3,2,1,0:T(2,128)} %broadcast_in_dim.14, s32[32]{0:T(128)S(1)} %get-tuple-element.178, f32[32,2,256]{2,1,0:T(2,128)S(1)} %copy.175), kind=kCustom, calls=%fused_computation.7 | custom fusion | bytes 196864 | tf_op jit(solution)/shard_map/scatter | solution.py:162
  109.7 5.0 %all-to-all-start.2 = ((f32[32,2,2,256]{3,2,1,0:T(2,128)}), f32[32,2,2,256]{3,2,1,0:T(2,128)S(1)}, u32[]{:S(2)}, u32[]{:S(2)}) async-start(f32[32,2,2,256]{3,2,1,0:T(2,128)} %scatter_fusion.1), calls=%async_computation.2 | async-start | bytes 262144 | tf_op jit(solution)/shard_map/all_to_all | solution.py:102
  115.7 7.3 %all-to-all-done.2 = f32[32,2,2,256]{3,2,1,0:T(2,128)S(1)} async-done(((f32[32,2,2,256]{3,2,1,0:T(2,128)}), f32[32,2,2,256]{3,2,1,0:T(2,128)S(1)}, u32[]{:S(2)}, u32[]{:S(2)}) %all-to-all-start.2) | async-done | bytes 131104 | tf_op jit(solution)/shard_map/all_to_all | solution.py:102
  124.0 1.3 %reshape.558 = f32[2,32,512]{2,1,0:T(8,128)} reshape(f32[2,2,16,32,16]{4,3,2,1,0:T(8,128)S(1)} %copy.177) | data formatting | bytes 262144 | tf_op jit(solution)/shard_map/reshape | solution.py:169
  (281 shorter events, 59.5 us)
Async XLA Ops:
  1.4 28.8 %collective-permute-start = (f32[16,4,128]{2,1,0:T(4,128)S(1)}, f32[16,4,128]{2,1,0:T(4,128)S(1)}, u32[]{:S(2)}, u32[]{:S(2)}) collective-permute-start(f32[16,4,128]{2,1,0:T(4,128)S(1)} %get-tuple-element.207), channel_id=1, source_target_pairs={{0,4},{4,8},{8,12},{12,16},{16,20},{20,24},{24,28},{28,0},{1,5},{5... | collective-permute-start | bytes 98312 | tf_op jit(solution)/shard_map/ppermute | solution.py:22
  4.4 25.9 %collective-permute-start.2 = (f32[16,4,128]{2,1,0:T(4,128)S(1)}, f32[16,4,128]{2,1,0:T(4,128)S(1)}, u32[]{:S(2)}, u32[]{:S(2)}) collective-permute-start(f32[16,4,128]{2,1,0:T(4,128)S(1)} %get-tuple-element.207), channel_id=1, source_target_pairs={{0,1},{1,2},{2,3},{3,0},{4,5},{5,6},{6,7},{7,4},{8,9},{9,10},{10,1... | collective-permute-start | bytes 98312 | tf_op jit(solution)/shard_map/ppermute | solution.py:22
  4.4 25.8 %collective-permute-start.1 = (f32[16,4,128]{2,1,0:T(4,128)S(1)}, f32[16,4,128]{2,1,0:T(4,128)S(1)}, u32[]{:S(2)}, u32[]{:S(2)}) collective-permute-start(f32[16,4,128]{2,1,0:T(4,128)S(1)} %get-tuple-element.206), channel_id=1, source_target_pairs={{4,0},{8,4},{12,8},{16,12},{20,16},{24,20},{28,24},{0,28},{5,1},{9... | collective-permute-start | bytes 98312 | tf_op jit(solution)/shard_map/ppermute | solution.py:23
  7.5 22.7 %collective-permute-start.3 = (f32[16,4,128]{2,1,0:T(4,128)S(1)}, f32[16,4,128]{2,1,0:T(4,128)S(1)}, u32[]{:S(2)}, u32[]{:S(2)}) collective-permute-start(f32[16,4,128]{2,1,0:T(4,128)S(1)} %get-tuple-element.206), channel_id=1, source_target_pairs={{1,0},{2,1},{3,2},{0,3},{5,4},{6,5},{7,6},{4,7},{9,8},{10,9},{11,1... | collective-permute-start | bytes 98312 | tf_op jit(solution)/shard_map/ppermute | solution.py:23
  8.9 0.7 copy-start.7
  9.9 0.7 copy-start.11
  10.6 6.0 %copy-start = (f32[32,4,128]{2,1,0:T(4,128)S(1)}, f32[32,4,128]{2,1,0:T(4,128)}, u32[]{:S(2)}) copy-start(f32[32,4,128]{2,1,0:T(4,128)} %param.21) | copy-start | bytes 196612
  13.3 10.3 %all-to-all-start = ((s32[32,1,2]{2,1,0:T(1,128)}), s32[32,1,2]{2,1,0:T(1,128)S(1)}, u32[]{:S(2)}, u32[]{:S(2)}) async-start(s32[32,1,2]{2,1,0:T(1,128)} %copy.152), calls=%async_computation | async-start | bytes 32768 | tf_op jit(solution)/shard_map/all_to_all | solution.py:94
  16.6 0.7 copy-start.8
  16.6 0.7 copy-start.9
  17.3 0.7 copy-start.10
  17.9 0.8 copy-start.5
  18.7 0.8 copy-start.6
  18.7 0.9 copy-start.4
  19.5 0.8 copy-start.3
  20.3 0.9 copy-start.2
  25.5 17.0 %all-to-all-start.1 = ((f32[32,2,2,256]{3,2,1,0:T(2,128)}), f32[32,2,2,256]{3,2,1,0:T(2,128)S(1)}, u32[]{:S(2)}, u32[]{:S(2)}) async-start(f32[32,2,2,256]{3,2,1,0:T(2,128)} %broadcast_multiply_fusion), calls=%async_computation.1 | async-start | bytes 262144 | tf_op jit(solution)/shard_map/all_to_all | solution.py:98
  41.4 0.8 copy-start.1
  44.9 6.7 %collective-permute-start.4 = (f32[16,4,128]{2,1,0:T(4,128)S(1)}, f32[16,4,128]{2,1,0:T(4,128)S(1)}, u32[]{:S(2)}, u32[]{:S(2)}) collective-permute-start(f32[16,4,128]{2,1,0:T(4,128)S(1)} %get-tuple-element.201), channel_id=1, source_target_pairs={{0,4},{4,8},{8,12},{12,16},{16,20},{20,24},{24,28},{28,0},{1,5},{5... | collective-permute-start | bytes 98312 | tf_op jit(solution)/shard_map/ppermute | solution.py:22
  46.7 5.0 %collective-permute-start.6 = (f32[16,4,128]{2,1,0:T(4,128)S(1)}, f32[16,4,128]{2,1,0:T(4,128)S(1)}, u32[]{:S(2)}, u32[]{:S(2)}) collective-permute-start(f32[16,4,128]{2,1,0:T(4,128)S(1)} %get-tuple-element.201), channel_id=1, source_target_pairs={{0,1},{1,2},{2,3},{3,0},{4,5},{5,6},{6,7},{7,4},{8,9},{9,10},{10,1... | collective-permute-start | bytes 98312 | tf_op jit(solution)/shard_map/ppermute | solution.py:22
  46.7 5.0 %collective-permute-start.5 = (f32[16,4,128]{2,1,0:T(4,128)S(1)}, f32[16,4,128]{2,1,0:T(4,128)S(1)}, u32[]{:S(2)}, u32[]{:S(2)}) collective-permute-start(f32[16,4,128]{2,1,0:T(4,128)S(1)} %get-tuple-element.200), channel_id=1, source_target_pairs={{4,0},{8,4},{12,8},{16,12},{20,16},{24,20},{28,24},{0,28},{5,1},{9... | collective-permute-start | bytes 98312 | tf_op jit(solution)/shard_map/ppermute | solution.py:23
  49.7 3.0 %collective-permute-start.7 = (f32[16,4,128]{2,1,0:T(4,128)S(1)}, f32[16,4,128]{2,1,0:T(4,128)S(1)}, u32[]{:S(2)}, u32[]{:S(2)}) collective-permute-start(f32[16,4,128]{2,1,0:T(4,128)S(1)} %get-tuple-element.200), channel_id=1, source_target_pairs={{1,0},{2,1},{3,2},{0,3},{5,4},{6,5},{7,6},{4,7},{9,8},{10,9},{11,1... | collective-permute-start | bytes 98312 | tf_op jit(solution)/shard_map/ppermute | solution.py:23
  64.4 6.7 %collective-permute-start.8 = (f32[16,4,128]{2,1,0:T(4,128)S(1)}, f32[16,4,128]{2,1,0:T(4,128)S(1)}, u32[]{:S(2)}, u32[]{:S(2)}) collective-permute-start(f32[16,4,128]{2,1,0:T(4,128)S(1)} %get-tuple-element.199), channel_id=1, source_target_pairs={{0,4},{4,8},{8,12},{12,16},{16,20},{20,24},{24,28},{28,0},{1,5},{5... | collective-permute-start | bytes 98312 | tf_op jit(solution)/shard_map/ppermute | solution.py:22
  64.8 7.6 %collective-permute-start.10 = (f32[16,4,128]{2,1,0:T(4,128)S(1)}, f32[16,4,128]{2,1,0:T(4,128)S(1)}, u32[]{:S(2)}, u32[]{:S(2)}) collective-permute-start(f32[16,4,128]{2,1,0:T(4,128)S(1)} %get-tuple-element.199), channel_id=1, source_target_pairs={{0,1},{1,2},{2,3},{3,0},{4,5},{5,6},{6,7},{7,4},{8,9},{9,10},{10,1... | collective-permute-start | bytes 98312 | tf_op jit(solution)/shard_map/ppermute | solution.py:22
  66.4 6.0 %collective-permute-start.9 = (f32[16,4,128]{2,1,0:T(4,128)S(1)}, f32[16,4,128]{2,1,0:T(4,128)S(1)}, u32[]{:S(2)}, u32[]{:S(2)}) collective-permute-start(f32[16,4,128]{2,1,0:T(4,128)S(1)} %get-tuple-element.198), channel_id=1, source_target_pairs={{4,0},{8,4},{12,8},{16,12},{20,16},{24,20},{28,24},{0,28},{5,1},{9... | collective-permute-start | bytes 98312 | tf_op jit(solution)/shard_map/ppermute | solution.py:23
  70.8 1.6 %collective-permute-start.11 = (f32[16,4,128]{2,1,0:T(4,128)S(1)}, f32[16,4,128]{2,1,0:T(4,128)S(1)}, u32[]{:S(2)}, u32[]{:S(2)}) collective-permute-start(f32[16,4,128]{2,1,0:T(4,128)S(1)} %get-tuple-element.198), channel_id=1, source_target_pairs={{1,0},{2,1},{3,2},{0,3},{5,4},{6,5},{7,6},{4,7},{9,8},{10,9},{11,1... | collective-permute-start | bytes 98312 | tf_op jit(solution)/shard_map/ppermute | solution.py:23
  84.2 7.0 %collective-permute-start.12 = (f32[16,4,128]{2,1,0:T(4,128)S(1)}, f32[16,4,128]{2,1,0:T(4,128)S(1)}, u32[]{:S(2)}, u32[]{:S(2)}) collective-permute-start(f32[16,4,128]{2,1,0:T(4,128)S(1)} %get-tuple-element.197), channel_id=1, source_target_pairs={{0,4},{4,8},{8,12},{12,16},{16,20},{20,24},{24,28},{28,0},{1,5},{5... | collective-permute-start | bytes 98312 | tf_op jit(solution)/shard_map/ppermute | solution.py:22
  84.3 7.8 %collective-permute-start.14 = (f32[16,4,128]{2,1,0:T(4,128)S(1)}, f32[16,4,128]{2,1,0:T(4,128)S(1)}, u32[]{:S(2)}, u32[]{:S(2)}) collective-permute-start(f32[16,4,128]{2,1,0:T(4,128)S(1)} %get-tuple-element.197), channel_id=1, source_target_pairs={{0,1},{1,2},{2,3},{3,0},{4,5},{5,6},{6,7},{7,4},{8,9},{9,10},{10,1... | collective-permute-start | bytes 98312 | tf_op jit(solution)/shard_map/ppermute | solution.py:22
  86.0 6.0 %collective-permute-start.13 = (f32[16,4,128]{2,1,0:T(4,128)S(1)}, f32[16,4,128]{2,1,0:T(4,128)S(1)}, u32[]{:S(2)}, u32[]{:S(2)}) collective-permute-start(f32[16,4,128]{2,1,0:T(4,128)S(1)} %get-tuple-element.196), channel_id=1, source_target_pairs={{4,0},{8,4},{12,8},{16,12},{20,16},{24,20},{28,24},{0,28},{5,1},{9... | collective-permute-start | bytes 98312 | tf_op jit(solution)/shard_map/ppermute | solution.py:23
  90.4 2.0 %collective-permute-start.15 = (f32[16,4,128]{2,1,0:T(4,128)S(1)}, f32[16,4,128]{2,1,0:T(4,128)S(1)}, u32[]{:S(2)}, u32[]{:S(2)}) collective-permute-start(f32[16,4,128]{2,1,0:T(4,128)S(1)} %get-tuple-element.196), channel_id=1, source_target_pairs={{1,0},{2,1},{3,2},{0,3},{5,4},{6,5},{7,6},{4,7},{9,8},{10,9},{11,1... | collective-permute-start | bytes 98312 | tf_op jit(solution)/shard_map/ppermute | solution.py:23
  109.7 13.3 %all-to-all-start.2 = ((f32[32,2,2,256]{3,2,1,0:T(2,128)}), f32[32,2,2,256]{3,2,1,0:T(2,128)S(1)}, u32[]{:S(2)}, u32[]{:S(2)}) async-start(f32[32,2,2,256]{3,2,1,0:T(2,128)} %scatter_fusion.1), calls=%async_computation.2 | async-start | bytes 262144 | tf_op jit(solution)/shard_map/all_to_all | solution.py:102
where the time goes:
time: 126 us; the launch traced here: 125 us
  starting transfers between devices  39.7 us (32%)
  matrix products  39.2 us (31%)
  local copies, waits for them, and re-layouts  26.7 us (21%)
  waiting for transfers between devices  13 us (10%)
  other arithmetic  4.73 us (4%)
  between operations  1.31 us (1%)
    dot_general x64, matrix products, select(): return jnp.einsum('kscg,ksgf->kscf', rows_here, picker, precision=HIGH)  37.4 us
    ppermute x8, starting transfers between devices, extended(): after = lax.ppermute(initial, axis, down)  18.1 us
    ppermute x8, starting transfers between devices, extended(): before = lax.ppermute(last, axis, up)  8.61 us
    all_to_all x1, waiting for transfers between devices, route_stress(): lax.all_to_all(returned, ('gx', 'gy'), split_axis=0, concat_axis=0, tiled...  7.32 us
    unnamed x38, local copies, waits for them, and re-layouts  6.33 us
    all_to_all x1, starting transfers between devices, route_stress(): lax.all_to_all(returned, ('gx', 'gy'), split_axis=0, concat_axis=0, tiled...  5.03 us
    all_to_all x1, starting transfers between devices, route_currents(): lax.all_to_all(served, ('gx', 'gy'), split_axis=0, concat_axis=0, tiled=T...  4.63 us
    gather x4, local copies, waits for them, and re-layouts, local(): partner = pick_lanes(pool[pool_index], lanes)  3.98 us
  transfers between devices with their start and end apart: 19, of which 9 were waited for; matrix products, arithmetic and copies ran while one was open for 15% of the time, Pallas kernels for 0%

commit v1 on v0

v1 whole, which is shorter than its diff:
```python
import functools
import jax
import jax.numpy as jnp
from jax import lax
from jax.experimental import pallas as pl
from jax.experimental.pallas import tpu as pltpu
from jax.sharding import PartitionSpec as P

PS = 16
EDGE = 16
NB = 4
NC = 4
NS = NB + NC
SUBSTEPS = 4
LANES = 128
PAD = 8
MESH = pl.DeviceIdType.MESH
F32 = jnp.float32
BF16 = jnp.bfloat16


def iota(shape, dim):
    return lax.broadcasted_iota(jnp.int32, shape, dim)


def split_bf16(value, parts):
    out = []
    for _ in range(parts):
        piece = value.astype(BF16)
        out.append(piece)
        value = value - piece.astype(F32)
    return out


def one_hot_dot(picks, values, parts):
    left = picks.astype(BF16)
    left = jnp.concatenate([left] * parts, axis=1)
    right = jnp.concatenate(split_bf16(values, parts), axis=0)
    return jnp.dot(left, right, preferred_element_type=F32)


def half_bit(shape):
    return (iota(shape, 1) // 32) % 2


def swap_halves(value):
    ahead = pltpu.roll(value, LANES - 32, 1)
    behind = pltpu.roll(value, 32, 1)
    return jnp.where(half_bit(value.shape) == 0, ahead, behind)


def to_row(column, count):
    eye = iota((count, count), 0) == iota((count, count), 1)
    return jnp.sum(jnp.where(eye, column, 0), axis=0, keepdims=True)


def kernel(
    cols,
    rows,
    blocks,
    row_of,
    source_of,
    ocean,
    state_in,
    code_row,
    source_col,
    cell,
    frac,
    bond_lanes,
    stiff_in,
    contact_lanes,
    state_out,
    stress_out,
    pool0,
    pool1,
    pool2,
    pool3,
    codes,
    outgoing,
    incoming,
    returned,
    arrived,
    turned,
    bond_index,
    contact_index,
    bond_got,
    contact_got,
    row_w,
    col_w,
    row_split,
    current,
    rank_b,
    pieces,
    stress,
    halo_send,
    halo_recv,
    all_send,
    all_recv,
):
    pools = (pool0, pool1, pool2, pool3)
    devices = cols * rows
    ax = lax.axis_index("gx")
    by = lax.axis_index("gy")
    me = ax * rows + by
    npy = ocean.shape[2] // PS

    def place_of(number):
        return (number // rows, lax.rem(number, rows))

    barrier = pltpu.get_barrier_semaphore()

    @pl.loop(1, devices)
    def _(i):
        pl.semaphore_signal(
            barrier, inc=1, device_id=place_of(lax.rem(me + i, devices)), device_id_type=MESH
        )

    codes[pl.ds(me, 1)] = code_row[...].reshape(1, 1, LANES)
    pool0[pl.ds(PAD, 4 * blocks), :] = state_in[...]
    for pool in pools:
        pool[pl.ds(0, PAD), :] = jnp.zeros((PAD, LANES), F32)
        pool[pl.ds(PAD + 4 * (blocks + 4 * EDGE), PAD), :] = jnp.zeros((PAD, LANES), F32)
    pl.semaphore_wait(barrier, devices - 1)

    def all_copy(source, target, which, number):
        return pltpu.make_async_remote_copy(
            src_ref=source,
            dst_ref=target,
            send_sem=all_send.at[which],
            recv_sem=all_recv.at[which],
            device_id=place_of(number),
            device_id_type=MESH,
        )

    other = lax.rem(me + 1, devices)

    @pl.loop(1, devices)
    def _(i):
        to = lax.rem(me + i, devices)
        all_copy(codes.at[pl.ds(me, 1)], codes.at[pl.ds(me, 1)], 0, to).start()

    def all_codes():
        part = codes.at[pl.ds(0, devices - 1)]
        return all_copy(part, part, 0, other)

    def all_blocks(outs, ins, which):
        size = 8 * (devices - 1)
        return all_copy(outs.at[pl.ds(0, size), :], outs.at[pl.ds(0, size), :], which, other)

    def send_blocks(outs, ins, which):
        mine = pl.ds(pl.multiple_of(me * 8, 8), 8)
        land = ins.at[me] if which == 1 else ins.at[mine, :]

        @pl.loop(1, devices)
        def _(i):
            to = lax.rem(me + i, devices)
            part = outs.at[pl.ds(pl.multiple_of(to * 8, 8), 8), :]
            all_copy(part, land, which, to).start()

        land[...] = outs[mine, :]

    last = PAD + 4 * (blocks - EDGE)
    targets = (
        (last, (lax.rem(ax + 1, cols), by)),
        (PAD, (lax.rem(ax + cols - 1, cols), by)),
        (last, (ax, lax.rem(by + 1, rows))),
        (PAD, (ax, lax.rem(by + rows - 1, rows))),
    )

    def halo(step):
        pool = pools[step]
        out = []
        for side, (start, device) in enumerate(targets):
            out.append(
                pltpu.make_async_remote_copy(
                    src_ref=pool.at[pl.ds(start, 4 * EDGE), :],
                    dst_ref=pool.at[pl.ds(PAD + 4 * (blocks + side * EDGE), 4 * EDGE), :],
                    send_sem=halo_send.at[step, side],
                    recv_sem=halo_recv.at[step, side],
                    device_id=device,
                    device_id_type=MESH,
                )
            )
        return out

    halos = [halo(step) for step in range(SUBSTEPS)]
    for copy in halos[0]:
        copy.start()

    lane = iota((npy, LANES), 1)
    tile = ocean[...]
    turn = jnp.concatenate(
        [tile[c, px * PS : (px + 1) * PS] for px in range(2) for c in range(2)] * 2, axis=0
    )
    turned[...] = turn.T
    columns = []
    for j in range(8):
        low = turned[pl.ds(j, npy, stride=PS), :]
        high = turned[pl.ds(8 + j, npy, stride=PS), :]
        columns.append(jnp.where(lane < 64, low, high))
    plain = jnp.concatenate(columns, axis=1)
    swapped = jnp.concatenate([swap_halves(c) for c in columns], axis=1)
    patches = jnp.concatenate([plain, swapped], axis=0)

    src = source_col[...]
    src_row = to_row(src, blocks)
    same = (src == src_row) & (iota((blocks, blocks), 1) < iota((blocks, blocks), 0))
    rank = jnp.sum(same.astype(jnp.int32), axis=1, keepdims=True)
    rank_b[...] = jnp.broadcast_to(rank, (blocks, LANES))
    rank_row = to_row(rank, blocks)
    owner = iota((devices, blocks), 0)
    homes = jnp.concatenate(
        [((src_row == owner) & (rank_row == r)).astype(F32) for r in range(2)], axis=0
    )

    quarter = iota((8, LANES), 0)
    ticks = iota((PS, LANES), 0)

    @pl.loop(0, blocks)
    def _(k):
        def line(ref, row):
            return ref[pl.ds(row, 1), :]

        for pair in range(NB // 2):
            first = line(bond_lanes, NB * k + 2 * pair)
            second = line(bond_lanes, NB * k + 2 * pair + 1)
            start = pl.multiple_of(16 * k + 8 * pair, 8)
            bond_index[pl.ds(start, 8), :] = jnp.where(quarter < 4, first, second)
        four = [line(contact_lanes, NC * k + s) for s in range(NC)]
        index = jnp.where(
            quarter < 4,
            jnp.where(quarter < 2, four[0], four[1]),
            jnp.where(quarter < 6, four[2], four[3]),
        )
        contact_index[pl.ds(pl.multiple_of(8 * k, 8), 8), :] = index
        i, j = line(cell, 2 * k), line(cell, 2 * k + 1)
        fx, fy = line(frac, 2 * k), line(frac, 2 * k + 1)
        col = jnp.where(ticks == i, 1.0 - fx, 0.0) + jnp.where(ticks == i + 1, fx, 0.0)
        row = jnp.where(ticks == j, 1.0 - fy, 0.0) + jnp.where(ticks == j + 1, fy, 0.0)
        at = pl.ds(pl.multiple_of(PS * k, PS), PS)
        col_w[at, :] = col
        row_w[at, :] = row
        high, low = split_bf16(row, 2)
        row_split[pl.ds(pl.multiple_of(2 * PS * k, 2 * PS), 2 * PS), :] = jnp.concatenate(
            [high, low], axis=0
        )

    all_codes().wait_recv()
    asked = codes[...].reshape(devices, LANES)
    match = (asked >= me * 64) & (asked < me * 64 + 64)
    spot = iota((devices, LANES), 1)
    first = jnp.min(jnp.where(match, spot, LANES), axis=1, keepdims=True)
    wish = jnp.where(match, asked - me * 64 + 1, 0)
    ids = [
        jnp.sum(jnp.where(spot == first, wish, 0), axis=1, keepdims=True) - 1,
        jnp.sum(jnp.where(spot == first, 0, wish), axis=1, keepdims=True) - 1,
    ]
    number = iota((devices, npy), 1)
    picks = jnp.concatenate(
        [
            jnp.concatenate(
                [(ids[r] == number + npy * px).astype(F32) for px in (r, 1 - r)], axis=1
            )
            for r in range(2)
        ],
        axis=0,
    )
    served = one_hot_dot(picks, patches, 3)
    wide = half_bit((devices, 8 * LANES)) == 0
    served = jnp.where(wide, served[:devices], served[devices:])
    for j in range(8):
        outgoing[pl.ds(j, devices, stride=8), :] = served[:, j * LANES : (j + 1) * LANES]
    send_blocks(outgoing, incoming, 1)
    id_rows = [to_row(one, devices) for one in ids]
    number = iota((npy, devices), 0)
    takes = jnp.concatenate(
        [
            jnp.concatenate(
                [(id_rows[r] == number + npy * px).astype(F32) for r in (px, 1 - px)], axis=1
            )
            for px in range(2)
        ],
        axis=0,
    )

    def own(step, c):
        return pools[step][pl.ds(PAD + c, blocks, stride=4), :]

    def forces(step):
        pool = pools[step]

        @pl.loop(0, blocks // 4)
        def _(group):
            for inner in range(4):
                k = 4 * group + inner
                for pair in range(NB // 2):
                    p = row_of[NS * k + 2 * pair]
                    q = row_of[NS * k + 2 * pair + 1]
                    low, high = pool[pl.ds(p + PAD, 8), :], pool[pl.ds(q + (PAD - 4), 8), :]
                    table = jnp.where(quarter < 4, low, high)
                    at = pl.ds(pl.multiple_of(16 * k + 8 * pair, 8), 8)
                    bond_got[at, :] = jnp.take_along_axis(
                        table, bond_index[at, :], axis=1, mode="promise_in_bounds"
                    )
                four = [
                    pool[pl.ds(row_of[NS * k + NB + s] + (PAD - 2 * s), 8), :]
                    for s in range(NC)
                ]
                table = jnp.where(
                    quarter < 4,
                    jnp.where(quarter < 2, four[0], four[1]),
                    jnp.where(quarter < 6, four[2], four[3]),
                )
                at = pl.ds(pl.multiple_of(8 * k, 8), 8)
                contact_got[at, :] = jnp.take_along_axis(
                    table, contact_index[at, :], axis=1, mode="promise_in_bounds"
                )

        x, y, u, v = [own(step, c) for c in range(4)]
        total_x = jnp.zeros((blocks, LANES), F32)
        total_y = jnp.zeros((blocks, LANES), F32)
        for s in range(NB):
            got = [bond_got[pl.ds(4 * s + c, blocks, stride=16), :] for c in range(4)]
            stiff = stiff_in[pl.ds(s, blocks, stride=NB), :]
            total_x += stiff * (got[0] - x) + 0.2 * (got[2] - u)
            total_y += stiff * (got[1] - y) + 0.2 * (got[3] - v)
        for s in range(NC):
            dx = contact_got[pl.ds(2 * s, blocks, stride=8), :] - x
            dy = contact_got[pl.ds(2 * s + 1, blocks, stride=8), :] - y
            dist = jnp.sqrt(dx * dx + dy * dy)
            push = 2.0 * jnp.maximum(1.5 - dist, 0.0) / jnp.maximum(dist, 0.5)
            total_x -= push * dx
            total_y -= push * dy
        return total_x, total_y

    def drag_of(step):
        slip_x = current[0] - own(step, 2)
        slip_y = current[1] - own(step, 3)
        half = 0.5 * jnp.sqrt(slip_x * slip_x + slip_y * slip_y)
        return half * slip_x, half * slip_y

    def advance(step, force, drag):
        u = own(step, 2) + 0.05 * (force[0] + drag[0])
        v = own(step, 3) + 0.05 * (force[1] + drag[1])
        x = own(step, 0) + 0.05 * u
        y = own(step, 1) + 0.05 * v
        return x, y, u, v

    def arrive(step):
        for copy in halos[step]:
            copy.wait_recv()

    arrive(0)
    force = forces(0)

    all_blocks(outgoing, incoming, 1).wait_recv()

    @pl.loop(0, blocks // 2)
    def _(group):
        for inner in range(2):
            k = 2 * group + inner
            values = incoming[source_of[k]]
            i = cell[pl.ds(2 * k, 1), :]
            fx = frac[pl.ds(2 * k, 1), :]
            base = jnp.broadcast_to(rank_b[pl.ds(k, 1), :] * 32 + i, (8, LANES))
            for c in range(2):
                total = jnp.zeros((8, LANES), F32)
                for h in range(2):
                    low, high = [
                        jnp.take_along_axis(
                            values, base + (h * 64 + c * 16 + d), axis=1, mode="promise_in_bounds"
                        )
                        for d in range(2)
                    ]
                    weight = row_w[pl.ds(pl.multiple_of(PS * k + 8 * h, 8), 8), :]
                    total += weight * ((1.0 - fx) * low + fx * high)
                current[c, pl.ds(k, 1), :] = jnp.sum(total, axis=0, keepdims=True)

    drag = drag_of(0)
    sum_x, sum_y = drag
    for step in range(SUBSTEPS - 1):
        if step > 0:
            arrive(step)
            force = forces(step)
        for c, value in enumerate(advance(step, force, drag)):
            pools[step + 1][pl.ds(PAD + c, blocks, stride=4), :] = value
        for copy in halos[step + 1]:
            copy.start()
        drag = drag_of(step + 1)
        sum_x, sum_y = sum_x + drag[0], sum_y + drag[1]

    stress[0] = sum_x * (-1.0 / SUBSTEPS)
    stress[1] = sum_y * (-1.0 / SUBSTEPS)
    low_half = iota((8, LANES), 1) < 64

    @pl.loop(0, blocks // 2)
    def _(group):
        for inner in range(2):
            k = 2 * group + inner
            col = col_w[pl.ds(pl.multiple_of(PS * k, PS), PS), :]
            spread = jnp.concatenate(
                [col * stress[0, pl.ds(k, 1), :], col * stress[1, pl.ds(k, 1), :]], axis=0
            )
            high, low = split_bf16(spread, 2)
            right = jnp.concatenate(
                [jnp.concatenate([high] * 4, axis=0), jnp.concatenate([low] * 4, axis=0)], axis=1
            )
            left = row_split[pl.ds(pl.multiple_of(2 * PS * k, 2 * PS), 2 * PS), :]
            left = jnp.concatenate([left, left], axis=1)
            piece = lax.dot_general(
                left, right, (((1,), (1,)), ((), ())), preferred_element_type=F32
            )
            piece = piece[:PS] + piece[PS:]
            pieces[pl.ds(pl.multiple_of(8 * k, 8), 8), :] = jnp.where(
                low_half, piece[:8], piece[8:]
            )

    gathered = jnp.concatenate([pieces[pl.ds(j, blocks, stride=8), :] for j in range(8)], axis=1)
    back = one_hot_dot(homes, gathered, 2)
    back = jnp.where(wide, back[:devices], back[devices:])
    for j in range(8):
        returned[pl.ds(j, devices, stride=8), :] = back[:, j * LANES : (j + 1) * LANES]
    send_blocks(returned, arrived, 2)

    arrive(SUBSTEPS - 1)
    force = forces(SUBSTEPS - 1)
    for c, value in enumerate(advance(SUBSTEPS - 1, force, drag)):
        state_out[pl.ds(c, blocks, stride=4), :] = value

    all_blocks(returned, arrived, 2).wait_recv()
    columns = [arrived[pl.ds(j, devices, stride=8), :] for j in range(8)]
    plain = jnp.concatenate(columns, axis=1)
    swapped = jnp.concatenate([swap_halves(c) for c in columns], axis=1)
    summed = one_hot_dot(takes, jnp.concatenate([plain, swapped], axis=0), 2)
    wide = half_bit((npy, 8 * LANES)) == 0
    summed = jnp.where(wide, summed[:npy], summed[npy:])
    for j in range(8):
        part = summed[:, j * LANES : (j + 1) * LANES]
        turned[pl.ds(j, npy, stride=PS), :] = part
        turned[pl.ds(8 + j, npy, stride=PS), :] = pltpu.roll(part, 64, 1)
    turn = turned[...].T
    for px in range(2):
        for c in range(2):
            start = (px * 2 + c) * PS
            stress_out[c, px * PS : (px + 1) * PS, :] = turn[start : start + PS]

    all_codes().wait_send()
    all_blocks(outgoing, incoming, 1).wait_send()
    all_blocks(returned, arrived, 2).wait_send()
    for step in range(SUBSTEPS):
        for copy in halos[step]:
            copy.wait_send()


def local(
    ocean_current,
    floe_state,
    floe_source,
    floe_patch,
    floe_cell,
    floe_frac,
    bond_blocks,
    bond_lanes,
    bond_stiff,
    contact_blocks,
    contact_lanes,
):
    cols = lax.axis_size("gx")
    rows = lax.axis_size("gy")
    devices = cols * rows
    blocks = floe_state.shape[0]
    region = jnp.concatenate([bond_blocks[:, 0], contact_blocks[:, 0]], axis=1)
    number = jnp.concatenate([bond_blocks[:, 1], contact_blocks[:, 1]], axis=1)
    start = jnp.where(region == 0, 0, blocks + EDGE * (region - 1))
    row_of = (4 * (start + number)).reshape(-1)
    source = floe_source[:, 0]
    code = (source * 64 + floe_patch[:, 0]).reshape(1, blocks)
    code = jnp.pad(code, ((0, 0), (0, LANES - blocks)), constant_values=-1)
    vmem = pl.BlockSpec(memory_space=pltpu.VMEM)
    smem = pl.BlockSpec(memory_space=pltpu.SMEM)
    tile = ocean_current.shape
    pool = pltpu.VMEM((2 * PAD + 4 * (blocks + 4 * EDGE), LANES), F32)
    swap = pltpu.VMEM((8 * devices, LANES), F32)
    state, ocean_stress = pl.pallas_call(
        functools.partial(kernel, cols, rows, blocks),
        out_shape=(
            jax.ShapeDtypeStruct((4 * blocks, LANES), F32),
            jax.ShapeDtypeStruct(tile, F32),
        ),
        in_specs=[smem, smem] + [vmem] * 9,
        out_specs=(vmem, vmem),
        scratch_shapes=[
            pool,
            pool,
            pool,
            pool,
            pltpu.VMEM((devices, 1, LANES), jnp.int32),
            swap,
            pltpu.VMEM((devices, 8, LANES), F32),
            swap,
            swap,
            pltpu.VMEM((tile[2], LANES), F32),
            pltpu.VMEM((16 * blocks, LANES), jnp.int32),
            pltpu.VMEM((8 * blocks, LANES), jnp.int32),
            pltpu.VMEM((16 * blocks, LANES), F32),
            pltpu.VMEM((8 * blocks, LANES), F32),
            pltpu.VMEM((PS * blocks, LANES), F32),
            pltpu.VMEM((PS * blocks, LANES), F32),
            pltpu.VMEM((2 * PS * blocks, LANES), BF16),
            pltpu.VMEM((2, blocks, LANES), F32),
            pltpu.VMEM((blocks, LANES), jnp.int32),
            pltpu.VMEM((8 * blocks, LANES), F32),
            pltpu.VMEM((2, blocks, LANES), F32),
            pltpu.SemaphoreType.DMA((SUBSTEPS, 4)),
            pltpu.SemaphoreType.DMA((SUBSTEPS, 4)),
            pltpu.SemaphoreType.DMA((3,)),
            pltpu.SemaphoreType.DMA((3,)),
        ],
        compiler_params=pltpu.CompilerParams(
            collective_id=0, has_side_effects=True, vmem_limit_bytes=32 * 1024 * 1024
        ),
    )(
        row_of,
        source,
        ocean_current,
        floe_state.reshape(4 * blocks, LANES),
        code,
        floe_source,
        floe_cell.reshape(2 * blocks, LANES),
        floe_frac.reshape(2 * blocks, LANES),
        bond_lanes.reshape(NB * blocks, LANES),
        bond_stiff.reshape(NB * blocks, LANES),
        contact_lanes.reshape(NC * blocks, LANES),
    )
    return (state.reshape(blocks, 4, LANES), ocean_stress)


def solution(mesh):
    whole = P(("gx", "gy"), None, None)
    flat = P(("gx", "gy"), None)
    ocean = P(None, "gx", "gy")
    in_specs = (ocean, whole, flat, flat) + (whole,) * 7
    return jax.shard_map(
        local, mesh=mesh, in_specs=in_specs, out_specs=(whole, ocean), check_vma=False
    )
```

time: 126 us -> 46.2 us (0.37)
  starting transfers between devices: 39.7 us -> 0 us
  matrix products: 39.2 us -> 0 us
  Pallas kernels: 0 us -> 37.4 us
  local copies, waits for them, and re-layouts: 26.7 us -> 6.96 us
  waiting for transfers between devices: 13 us -> 0 us
  other arithmetic: 4.73 us -> 0.72 us
    dot_general x67 -> x0, matrix products: 39.2 us -> none  [the longest x64 37.4 us: select(): return jnp.einsum('kscg,ksgf->kscf', rows_here, picker, precision=HIGH)]
    pallas_call x0 -> x1, Pallas kernels: none -> 37.4 us  [local(): pl.pallas_call(functools.partial(kernel, cols, rows, blocks), out_shape=(...]
    ppermute x16 -> x0, starting transfers between devices: 26.7 us -> none  [the longest x8 18.1 us: extended(): after = lax.ppermute(initial, axis, down)]
    all_to_all x3 -> x0, starting transfers between devices: 12.9 us -> none  [the longest x1 5.03 us: route_stress(): lax.all_to_all(returned, ('gx', 'gy'), split_axis=0, concat_axis=0, tiled...]
    all_to_all x3 -> x0, waiting for transfers between devices: 8.54 us -> none  [the longest x1 7.32 us: route_stress(): lax.all_to_all(returned, ('gx', 'gy'), split_axis=0, concat_axis=0, tiled...]
    scatter x2 -> x0, local copies, waits for them, and re-layouts: 5.81 us -> none  [the longest x1 3.79 us: local(): jnp.zeros((devices, capacity, 2, PS * PS), jnp.float32).at[source, rank]]
    gather x7 -> x0, local copies, waits for them, and re-layouts: 5.5 us -> none  [the longest x4 3.98 us: local(): partner = pick_lanes(pool[pool_index], lanes)]
    ppermute x16 -> x0, waiting for transfers between devices: 4.48 us -> none  [the longest x8 3.35 us: extended(): after = lax.ppermute(initial, axis, down)]
  transfers between devices with their start and end apart: 19 -> 0, of which waited for: 9 -> 0; matrix products, arithmetic and copies ran while one was open for 15% -> 0% of each run, Pallas kernels for 0% -> 0%
where the time goes in v1:
time: 46.2 us; the launch traced here: 45.8 us
  Pallas kernels  37.4 us (81%)
  local copies, waits for them, and re-layouts  6.96 us (15%)
  other arithmetic  0.72 us (2%)
  between operations  0.66 us (1%)
    pallas_call x1, Pallas kernels, local(): pl.pallas_call(functools.partial(kernel, cols, rows, blocks), out_shape=(...  37.4 us
    unnamed x19, local copies, waits for them, and re-layouts  6.05 us

profile of v1, /device:TPU:0, one launch (start us, length us, event | category | flops | bytes accessed | tf_op | source)
XLA Modules:
  0.0 45.8 jit_solution(3870562222288869775)
XLA Ops:
  0.6 0.0 copy-start.1
  0.6 0.7 %add_bitcast_fusion = s32[1,32]{1,0:T(1,128)S(1)} fusion(s32[32,1]{0,1:T(1,128)} %param.14, s32[32,1]{0,1:T(1,128)} %param.13), kind=kLoop, calls=%fused_computation.7 | loop fusion | flops 64 | bytes 384 | tf_op jit(solution)/shard_map/add | solution.py:477
  1.4 0.7 %slice_bitcast_fusion.2 = (s32[32,4]{0,1:T(4,128)S(1)}, s32[32,4]{0,1:T(4,128)S(1)}, s32[32,4]{0,1:T(4,128)S(1)}, s32[32,4]{0,1:T(4,128)S(1)}) fusion(s32[32,2,4]{0,2,1:T(4,128)} %param.20, s32[32,2,4]{0,2,1:T(4,128)} %param.17), kind=kLoop, calls=%fused_computation.5 | loop fusion | bytes 4096 | tf_op jit(solution)/shard_map/squeeze | solution.py:472
  2.1 0.0 copy-start.7
  2.1 0.0 copy-start.5
  2.1 0.1 copy.14
  2.2 0.1 reshape.71.row_of
  2.3 0.5 %copy-done.7 = s32[32,1]{0,1:T(1,128)S(1)} copy-done((s32[32,1]{0,1:T(1,128)S(1)}, s32[32,1]{0,1:T(1,128)}, u32[]{:S(2)}) %copy-start.7) | copy-done | bytes 152
  2.7 0.1 copy.15.source_col
  2.8 0.0 copy-done.1
  2.8 0.0 copy-done.5
  2.9 0.0 copy-start
  2.9 0.9 %copy-done = f32[2,32,512]{2,1,0:T(8,128)S(1)} copy-done((f32[2,32,512]{2,1,0:T(8,128)S(1)}, f32[2,32,512]{2,1,0:T(8,128)}, u32[]{:S(2)}) %copy-start) | copy-done | bytes 131096
  3.8 0.0 copy-start.2
  3.8 0.8 %copy-done.2 = s32[32,4,128]{2,1,0:T(4,128)S(1)} copy-done((s32[32,4,128]{2,1,0:T(4,128)S(1)}, s32[32,4,128]{2,1,0:T(4,128)}, u32[]{:S(2)}) %copy-start.2) | copy-done | bytes 65560
  4.6 0.0 copy-start.3
  4.6 0.8 %copy-done.3 = f32[32,4,128]{2,1,0:T(4,128)S(1)} copy-done((f32[32,4,128]{2,1,0:T(4,128)S(1)}, f32[32,4,128]{2,1,0:T(4,128)}, u32[]{:S(2)}) %copy-start.3) | copy-done | bytes 65560
  5.4 0.0 copy-start.4
  5.4 0.8 %copy-done.4 = s32[32,4,128]{2,1,0:T(4,128)S(1)} copy-done((s32[32,4,128]{2,1,0:T(4,128)S(1)}, s32[32,4,128]{2,1,0:T(4,128)}, u32[]{:S(2)}) %copy-start.4) | copy-done | bytes 65560
  6.3 0.0 copy-start.6
  6.3 0.8 %copy-done.6 = f32[32,2,128]{2,1,0:T(2,128)S(1)} copy-done((f32[32,2,128]{2,1,0:T(2,128)S(1)}, f32[32,2,128]{2,1,0:T(2,128)}, u32[]{:S(2)}) %copy-start.6) | copy-done | bytes 32792
  7.0 37.4 %shard_map.122 = (f32[128,128]{1,0:T(8,128)S(1)}, f32[2,32,512]{2,1,0:T(8,128)S(1)}) custom-call(s32[256]{0:T(256)S(1)} %reshape.71.row_of, s32[32]{0:T(128)S(1)} %bitcast.25, f32[2,32,512]{2,1,0:T(8,128)S(1)} %copy-done, f32[128,128]{1,0:T(8,128)S(1)} %bitcast.19, s32[1,128]{1,0:T(1,128)S(1)} %pad.4.code_row, s32[32,1]{1,0:T(8,128)S(1)} %copy.15.source_col, ...), custom_call_target="tpu_custom_call" | custom-call | tf_op jit(solution)/shard_map/pallas_call | solution.py:484
  44.5 0.6 %copy.18 = f32[32,4,128]{2,1,0:T(4,128)} copy(f32[32,4,128]{2,1,0:T(4,128)S(1)} %bitcast.18) | data formatting | bytes 131072
  45.1 0.7 %copy.19 = f32[2,32,512]{2,1,0:T(8,128)} copy(f32[2,32,512]{2,1,0:T(8,128)S(1)} %get-tuple-element.15) | data formatting | bytes 262144
  (2 shorter events, 0.0 us)
Async XLA Ops:
  0.6 2.2 %copy-start.1 = (f32[32,4,128]{2,1,0:T(4,128)S(1)}, f32[32,4,128]{2,1,0:T(4,128)}, u32[]{:S(2)}) copy-start(f32[32,4,128]{2,1,0:T(4,128)} %param.12) | copy-start | bytes 196612
  2.1 0.7 %copy-start.7 = (s32[32,1]{0,1:T(1,128)S(1)}, s32[32,1]{0,1:T(1,128)}, u32[]{:S(2)}) copy-start(s32[32,1]{0,1:T(1,128)} %param.13) | copy-start | bytes 388
  2.1 0.8 %copy-start.5 = (s32[32,2,128]{2,1,0:T(2,128)S(1)}, s32[32,2,128]{2,1,0:T(2,128)}, u32[]{:S(2)}) copy-start(s32[32,2,128]{2,1,0:T(2,128)} %param.15) | copy-start | bytes 98308
  2.9 0.9 %copy-start = (f32[2,32,512]{2,1,0:T(8,128)S(1)}, f32[2,32,512]{2,1,0:T(8,128)}, u32[]{:S(2)}) copy-start(f32[2,32,512]{2,1,0:T(8,128)} %ocean.1) | copy-start | bytes 393220
  3.8 0.8 %copy-start.2 = (s32[32,4,128]{2,1,0:T(4,128)S(1)}, s32[32,4,128]{2,1,0:T(4,128)}, u32[]{:S(2)}) copy-start(s32[32,4,128]{2,1,0:T(4,128)} %param.18) | copy-start | bytes 196612
  4.6 0.8 %copy-start.3 = (f32[32,4,128]{2,1,0:T(4,128)S(1)}, f32[32,4,128]{2,1,0:T(4,128)}, u32[]{:S(2)}) copy-start(f32[32,4,128]{2,1,0:T(4,128)} %param.19) | copy-start | bytes 196612
  5.4 0.8 %copy-start.4 = (s32[32,4,128]{2,1,0:T(4,128)S(1)}, s32[32,4,128]{2,1,0:T(4,128)}, u32[]{:S(2)}) copy-start(s32[32,4,128]{2,1,0:T(4,128)} %param.21) | copy-start | bytes 196612
  6.3 0.8 %copy-start.6 = (f32[32,2,128]{2,1,0:T(2,128)S(1)}, f32[32,2,128]{2,1,0:T(2,128)}, u32[]{:S(2)}) copy-start(f32[32,2,128]{2,1,0:T(2,128)} %param.16) | copy-start | bytes 98308

commit v2 on v1

--- a/solution.py
+++ b/solution.py
@@ -54,23 +54,41 @@
     return jnp.sum(jnp.where(eye, column, 0), axis=0, keepdims=True)
 
 
+def to_column(row, count):
+    eye = iota((count, count), 0) == iota((count, count), 1)
+    return jnp.sum(jnp.where(eye, row, 0), axis=1, keepdims=True)
+
+
 def kernel(
     cols,
     rows,
     blocks,
-    row_of,
+    bond_blocks,
+    contact_blocks,
     source_of,
+    source_row,
+    patch_row,
+    state_far,
+    ocean_far,
+    cell_far,
+    frac_far,
+    bond_far,
+    contact_far,
+    stiff_far,
+    state_out,
+    stress_out,
     ocean,
-    state_in,
-    code_row,
-    source_col,
     cell,
     frac,
     bond_lanes,
+    contact_lanes,
     stiff_in,
-    contact_lanes,
-    state_out,
-    stress_out,
+    row_of,
+    fetch_sem,
+    patches,
+    state_near,
+    stress_near,
+    store_sem,
     pool0,
     pool1,
     pool2,
@@ -104,40 +122,58 @@
     me = ax * rows + by
     npy = ocean.shape[2] // PS
 
-    def place_of(number):
-        return (number // rows, lax.rem(number, rows))
+    own_state = pl.ds(PAD, 4 * blocks)
+    fetches = [
+        pltpu.make_async_copy(far, near, fetch_sem.at[n])
+        for n, (far, near) in enumerate(
+            (
+                (state_far, pool0.at[own_state, :]),
+                (ocean_far, ocean),
+                (bond_far, bond_lanes),
+                (contact_far, contact_lanes),
+                (cell_far, cell),
+                (frac_far, frac),
+                (stiff_far, stiff_in),
+            )
+        )
+    ]
+    for copy in fetches:
+        copy.start()
+
+    def wrap(value, size):
+        return jnp.where(value >= size, value - size, value)
+
+    to_a = [wrap(ax + i, cols) for i in range(cols)]
+    to_b = [wrap(by + j, rows) for j in range(rows)]
+    others = [(to_a[i], to_b[j]) for i in range(cols) for j in range(rows) if i or j]
 
     barrier = pltpu.get_barrier_semaphore()
-
-    @pl.loop(1, devices)
-    def _(i):
-        pl.semaphore_signal(
-            barrier, inc=1, device_id=place_of(lax.rem(me + i, devices)), device_id_type=MESH
-        )
-
-    codes[pl.ds(me, 1)] = code_row[...].reshape(1, 1, LANES)
-    pool0[pl.ds(PAD, 4 * blocks), :] = state_in[...]
+    for device in others:
+        pl.semaphore_signal(barrier, inc=1, device_id=device, device_id_type=MESH)
+
+    src_row = source_row[...]
+    code = jnp.full((1, LANES - blocks), -1, jnp.int32)
+    code = jnp.concatenate([src_row * 64 + patch_row[...], code], axis=1)
+    codes[pl.ds(me, 1)] = code.reshape(1, 1, LANES)
     for pool in pools:
         pool[pl.ds(0, PAD), :] = jnp.zeros((PAD, LANES), F32)
         pool[pl.ds(PAD + 4 * (blocks + 4 * EDGE), PAD), :] = jnp.zeros((PAD, LANES), F32)
     pl.semaphore_wait(barrier, devices - 1)
 
-    def all_copy(source, target, which, number):
+    def all_copy(source, target, which, device):
         return pltpu.make_async_remote_copy(
             src_ref=source,
             dst_ref=target,
             send_sem=all_send.at[which],
             recv_sem=all_recv.at[which],
-            device_id=place_of(number),
+            device_id=device,
             device_id_type=MESH,
         )
 
-    other = lax.rem(me + 1, devices)
-
-    @pl.loop(1, devices)
-    def _(i):
-        to = lax.rem(me + i, devices)
-        all_copy(codes.at[pl.ds(me, 1)], codes.at[pl.ds(me, 1)], 0, to).start()
+    other = others[0]
+
+    for device in others:
+        all_copy(codes.at[pl.ds(me, 1)], codes.at[pl.ds(me, 1)], 0, device).start()
 
     def all_codes():
         part = codes.at[pl.ds(0, devices - 1)]
@@ -151,20 +187,19 @@
         mine = pl.ds(pl.multiple_of(me * 8, 8), 8)
         land = ins.at[me] if which == 1 else ins.at[mine, :]
 
-        @pl.loop(1, devices)
-        def _(i):
-            to = lax.rem(me + i, devices)
+        for device in others:
+            to = device[0] * rows + device[1]
             part = outs.at[pl.ds(pl.multiple_of(to * 8, 8), 8), :]
-            all_copy(part, land, which, to).start()
+            all_copy(part, land, which, device).start()
 
         land[...] = outs[mine, :]
 
     last = PAD + 4 * (blocks - EDGE)
     targets = (
-        (last, (lax.rem(ax + 1, cols), by)),
-        (PAD, (lax.rem(ax + cols - 1, cols), by)),
-        (last, (ax, lax.rem(by + 1, rows))),
-        (PAD, (ax, lax.rem(by + rows - 1, rows))),
+        (last, (to_a[1], by)),
+        (PAD, (to_a[-1], by)),
+        (last, (ax, to_b[1])),
+        (PAD, (ax, to_b[-1])),
     )
 
     def halo(step):
@@ -184,9 +219,12 @@
         return out
 
     halos = [halo(step) for step in range(SUBSTEPS)]
+    fetches[0].wait()
     for copy in halos[0]:
         copy.start()
 
+    for copy in fetches[1:]:
+        copy.wait()
     lane = iota((npy, LANES), 1)
     tile = ocean[...]
     turn = jnp.concatenate(
@@ -200,10 +238,11 @@
         columns.append(jnp.where(lane < 64, low, high))
     plain = jnp.concatenate(columns, axis=1)
     swapped = jnp.concatenate([swap_halves(c) for c in columns], axis=1)
-    patches = jnp.concatenate([plain, swapped], axis=0)
-
-    src = source_col[...]
-    src_row = to_row(src, blocks)
+    patches[...] = jnp.concatenate(
+        split_bf16(jnp.concatenate([plain, swapped], axis=0), 3), axis=0
+    )
+
+    src = to_column(src_row, blocks)
     same = (src == src_row) & (iota((blocks, blocks), 1) < iota((blocks, blocks), 0))
     rank = jnp.sum(same.astype(jnp.int32), axis=1, keepdims=True)
     rank_b[...] = jnp.broadcast_to(rank, (blocks, LANES))
@@ -218,6 +257,12 @@
 
     @pl.loop(0, blocks)
     def _(k):
+        for s in range(NS):
+            table = bond_blocks if s < NB else contact_blocks
+            region = table[0, s % NB, k]
+            start = jnp.where(region == 0, 0, blocks + EDGE * (region - 1))
+            row_of[NS * k + s] = 4 * (start + table[1, s % NB, k])
+
         def line(ref, row):
             return ref[pl.ds(row, 1), :]
 
@@ -265,7 +310,8 @@
         ],
         axis=0,
     )
-    served = one_hot_dot(picks, patches, 3)
+    picks = jnp.concatenate([picks.astype(BF16)] * 3, axis=1)
+    served = jnp.dot(picks, patches[...], preferred_element_type=F32)
     wide = half_bit((devices, 8 * LANES)) == 0
     served = jnp.where(wide, served[:devices], served[devices:])
     for j in range(8):
@@ -289,10 +335,10 @@
     def forces(step):
         pool = pools[step]
 
-        @pl.loop(0, blocks // 4)
+        @pl.loop(0, blocks // 8)
         def _(group):
-            for inner in range(4):
-                k = 4 * group + inner
+            for inner in range(8):
+                k = 8 * group + inner
                 for pair in range(NB // 2):
                     p = row_of[NS * k + 2 * pair]
                     q = row_of[NS * k + 2 * pair + 1]
@@ -355,11 +401,11 @@
 
     all_blocks(outgoing, incoming, 1).wait_recv()
 
-    @pl.loop(0, blocks // 2)
+    @pl.loop(0, blocks // 8)
     def _(group):
-        for inner in range(2):
-            k = 2 * group + inner
-            values = incoming[source_of[k]]
+        for inner in range(8):
+            k = 8 * group + inner
+            values = incoming[source_of[0, k]]
             i = cell[pl.ds(2 * k, 1), :]
             fx = frac[pl.ds(2 * k, 1), :]
             base = jnp.broadcast_to(rank_b[pl.ds(k, 1), :] * 32 + i, (8, LANES))
@@ -393,10 +439,10 @@
     stress[1] = sum_y * (-1.0 / SUBSTEPS)
     low_half = iota((8, LANES), 1) < 64
 
-    @pl.loop(0, blocks // 2)
+    @pl.loop(0, blocks // 8)
     def _(group):
-        for inner in range(2):
-            k = 2 * group + inner
+        for inner in range(8):
+            k = 8 * group + inner
             col = col_w[pl.ds(pl.multiple_of(PS * k, PS), PS), :]
             spread = jnp.concatenate(
                 [col * stress[0, pl.ds(k, 1), :], col * stress[1, pl.ds(k, 1), :]], axis=0
@@ -425,7 +471,9 @@
     arrive(SUBSTEPS - 1)
     force = forces(SUBSTEPS - 1)
     for c, value in enumerate(advance(SUBSTEPS - 1, force, drag)):
-        state_out[pl.ds(c, blocks, stride=4), :] = value
+        state_near[pl.ds(c, blocks, stride=4), :] = value
+    store_state = pltpu.make_async_copy(state_near, state_out, store_sem.at[0])
+    store_state.start()
 
     all_blocks(returned, arrived, 2).wait_recv()
     columns = [arrived[pl.ds(j, devices, stride=8), :] for j in range(8)]
@@ -442,7 +490,9 @@
     for px in range(2):
         for c in range(2):
             start = (px * 2 + c) * PS
-            stress_out[c, px * PS : (px + 1) * PS, :] = turn[start : start + PS]
+            stress_near[c, px * PS : (px + 1) * PS, :] = turn[start : start + PS]
+    store_stress = pltpu.make_async_copy(stress_near, stress_out, store_sem.at[1])
+    store_stress.start()
 
     all_codes().wait_send()
     all_blocks(outgoing, incoming, 1).wait_send()
@@ -450,6 +500,8 @@
     for step in range(SUBSTEPS):
         for copy in halos[step]:
             copy.wait_send()
+    store_state.wait()
+    store_stress.wait()
 
 
 def local(
@@ -469,16 +521,11 @@
     rows = lax.axis_size("gy")
     devices = cols * rows
     blocks = floe_state.shape[0]
-    region = jnp.concatenate([bond_blocks[:, 0], contact_blocks[:, 0]], axis=1)
-    number = jnp.concatenate([bond_blocks[:, 1], contact_blocks[:, 1]], axis=1)
-    start = jnp.where(region == 0, 0, blocks + EDGE * (region - 1))
-    row_of = (4 * (start + number)).reshape(-1)
-    source = floe_source[:, 0]
-    code = (source * 64 + floe_patch[:, 0]).reshape(1, blocks)
-    code = jnp.pad(code, ((0, 0), (0, LANES - blocks)), constant_values=-1)
     vmem = pl.BlockSpec(memory_space=pltpu.VMEM)
     smem = pl.BlockSpec(memory_space=pltpu.SMEM)
+    far = pl.BlockSpec(memory_space=pltpu.HBM)
     tile = ocean_current.shape
+    ints = jnp.int32
     pool = pltpu.VMEM((2 * PAD + 4 * (blocks + 4 * EDGE), LANES), F32)
     swap = pltpu.VMEM((8 * devices, LANES), F32)
     state, ocean_stress = pl.pallas_call(
@@ -487,9 +534,21 @@
             jax.ShapeDtypeStruct((4 * blocks, LANES), F32),
             jax.ShapeDtypeStruct(tile, F32),
         ),
-        in_specs=[smem, smem] + [vmem] * 9,
-        out_specs=(vmem, vmem),
+        in_specs=[smem] * 3 + [vmem] * 2 + [far] * 7,
+        out_specs=(far, far),
         scratch_shapes=[
+            pltpu.VMEM(tile, F32),
+            pltpu.VMEM((2 * blocks, LANES), ints),
+            pltpu.VMEM((2 * blocks, LANES), F32),
+            pltpu.VMEM((NB * blocks, LANES), ints),
+            pltpu.VMEM((NC * blocks, LANES), ints),
+            pltpu.VMEM((NB * blocks, LANES), F32),
+            pltpu.SMEM((NS * blocks,), ints),
+            pltpu.SemaphoreType.DMA((7,)),
+            pltpu.VMEM((6 * (tile[2] // PS), 8 * LANES), BF16),
+            pltpu.VMEM((4 * blocks, LANES), F32),
+            pltpu.VMEM(tile, F32),
+            pltpu.SemaphoreType.DMA((2,)),
             pool,
             pool,
             pool,
@@ -517,20 +576,21 @@
             pltpu.SemaphoreType.DMA((3,)),
         ],
         compiler_params=pltpu.CompilerParams(
-            collective_id=0, has_side_effects=True, vmem_limit_bytes=32 * 1024 * 1024
+            collective_id=0, has_side_effects=True, vmem_limit_bytes=63 * 1024 * 1024
         ),
     )(
-        row_of,
-        source,
+        bond_blocks.transpose(1, 2, 0),
+        contact_blocks.transpose(1, 2, 0),
+        floe_source.T,
+        floe_source.T,
+        floe_patch.T,
+        floe_state.reshape(4 * blocks, LANES),
         ocean_current,
-        floe_state.reshape(4 * blocks, LANES),
-        code,
-        floe_source,
         floe_cell.reshape(2 * blocks, LANES),
         floe_frac.reshape(2 * blocks, LANES),
         bond_lanes.reshape(NB * blocks, LANES),
+        contact_lanes.reshape(NC * blocks, LANES),
         bond_stiff.reshape(NB * blocks, LANES),
-        contact_lanes.reshape(NC * blocks, LANES),
     )
     return (state.reshape(blocks, 4, LANES), ocean_stress)
 

time: 46.2 us -> 38.2 us (0.83)
  local copies, waits for them, and re-layouts: 6.96 us -> 2.17 us
  Pallas kernels: 37.4 us -> 35.2 us
  other arithmetic: 0.72 us -> 0 us
    unnamed x19 -> x4, local copies, waits for them, and re-layouts: 6.05 us -> 2.17 us
    pallas_call x1, Pallas kernels: 37.4 us -> 35.2 us  [local(): pl.pallas_call(functools.partial(kernel, cols, rows, blocks), out_shape=(...]
    squeeze x1 -> x0, local copies, waits for them, and re-layouts: 0.73 us -> none  [local(): region = jnp.concatenate([bond_blocks[:, 0], contact_blocks[:, 0]], axis=1)]
    add x1 -> x0, other arithmetic: 0.71 us -> none  [local(): code = (source * 64 + floe_patch[:, 0]).reshape(1, blocks)]
where the time goes in v2:
time: 38.2 us; the launch traced here: 38 us
  Pallas kernels  35.2 us (92%)
  local copies, waits for them, and re-layouts  2.17 us (6%)
  between operations  0.65 us (2%)
    pallas_call x1, Pallas kernels, local(): pl.pallas_call(functools.partial(kernel, cols, rows, blocks), out_shape=(...  35.2 us
    unnamed x4, local copies, waits for them, and re-layouts  2.17 us

profile of v2, /device:TPU:0, one launch (start us, length us, event | category | flops | bytes accessed | tf_op | source)
XLA Modules:
  0.0 38.0 jit_solution(10759492833687099780)
XLA Ops:
  0.6 35.2 %shard_map.122 = (f32[128,128]{1,0:T(8,128)}, f32[2,32,512]{2,1,0:T(8,128)}) custom-call(s32[2,4,32]{2,1,0:T(4,128)} %bitcast.18, s32[2,4,32]{2,1,0:T(4,128)} %bitcast.19, s32[1,32]{1,0:T(1,128)} %bitcast.20, s32[1,32]{1,0:T(1,128)} %bitcast.21, s32[1,32]{1,0:T(1,128)} %bitcast.22, f32[128,128]{1,0:T(8,128)} %bitcast.12, f32[2,32,512]{2,1,0:T(8,128)} %ocean_far.1, ...), custom_call_target="tpu_custom_call" | custom-call | tf_op jit(solution)/shard_map/pallas_call | solution.py:531
  35.8 0.0 copy-start
  35.8 1.5 %copy.15 = f32[32,4,128]{2,1,0:T(4,128)} copy(f32[32,4,128]{2,1,0:T(4,128)} %bitcast.11) | data formatting | bytes 131072
  37.4 0.0 copy-done
  37.4 0.7 %copy.16 = f32[2,32,512]{2,1,0:T(8,128)} copy(f32[2,32,512]{2,1,0:T(8,128)S(1)} %copy-done) | data formatting | bytes 262144
Async XLA Ops:
  35.8 1.5 %copy-start = (f32[2,32,512]{2,1,0:T(8,128)S(1)}, f32[2,32,512]{2,1,0:T(8,128)}, u32[]{:S(2)}) copy-start(f32[2,32,512]{2,1,0:T(8,128)} %get-tuple-element.9) | copy-start | bytes 393220
